TPU v7x, 768 devices: a whole 4x8x12 slice. The times are simulated.
768 devices in a mesh: fsdp: 96 (over y, z_hi, x), tp: 8 (over z_lo, core).
Axes of the slice: x: 4, y: 8, z: 12 (z_hi: 3, z_lo: 4; z = z_hi * 4 + z_lo), core: 2. Of those that a mesh axis runs over, the one named last changes fastest.
Arguments:
- tokens: bfloat16 [288, 8192], P('fsdp', 'tp'), may hold values from -6 to 6
- grad_out: bfloat16 [288, 8192], P('fsdp', 'tp'), may hold values from -6 to 6
- gate_codes: bfloat16 [8192, 36864], P('tp', 'fsdp'), may hold values from -0.0625 to 0.0625
- gate_scale: float32 [64, 288], P('tp', 'fsdp'), may hold values from 0.25 to 4
- up_codes: bfloat16 [8192, 36864], P('tp', 'fsdp'), may hold values from -0.0625 to 0.0625
- up_scale: float32 [64, 288], P('tp', 'fsdp'), may hold values from 0.25 to 4
- down_codes: bfloat16 [36864, 8192], P('fsdp', 'tp'), may hold values from -0.03125 to 0.03125
- down_scale: float32 [288, 64], P('fsdp', 'tp'), may hold values from 0.25 to 4
Outputs:
- grad_tokens: bfloat16 [288, 8192], P('fsdp', 'tp')
- grad_gate: bfloat16 [8192, 36864], P('tp', 'fsdp')
- grad_up: bfloat16 [8192, 36864], P('tp', 'fsdp')
- grad_down: bfloat16 [36864, 8192], P('fsdp', 'tp')
All inputs are finite; a program needn't handle non-finite values.
Results may differ from a plain program's by a relative error of at most 0.0072.
Values may be sent and summed in bfloat16 or wider, within the bound.
A program may use at most 32 MiB of HBM per device.

v0:
```python
import jax
import jax.numpy as jnp
from jax import lax
from jax.sharding import PartitionSpec as P


def dequantize(codes, scales):
    blocks_down, blocks_across = scales.shape
    tile_rows = codes.shape[0] // blocks_down
    tile_cols = codes.shape[1] // blocks_across
    scaled = (
        codes.astype(jnp.float32).reshape(blocks_down, tile_rows, blocks_across, tile_cols)
        * scales[:, None, :, None]
    )
    return scaled.reshape(codes.shape).astype(jnp.bfloat16)


def contract(left, right, left_dim, right_dim):
    return lax.dot_general(
        left, right, (((left_dim,), (right_dim,)), ((), ())), preferred_element_type=jnp.float32
    )


def swiglu_back(gate, up_value, grad_hidden):
    sigma = jax.nn.sigmoid(gate)
    active = gate * sigma
    hidden = (active * up_value).astype(jnp.bfloat16)
    grad_up_pre = (grad_hidden * active).astype(jnp.bfloat16)
    grad_gate_pre = (grad_hidden * up_value * sigma * (1.0 + gate * (1.0 - sigma))).astype(
        jnp.bfloat16
    )
    return (hidden, grad_gate_pre, grad_up_pre)


def local(tokens, grad_out, gate_codes, gate_scale, up_codes, up_scale, down_codes, down_scale):
    gate_weight = dequantize(gate_codes, gate_scale)
    up_weight = dequantize(up_codes, up_scale)
    down_weight = dequantize(down_codes, down_scale)
    inputs, cotangent = (
        lax.all_gather(tokens, "fsdp", axis=0, tiled=True),
        lax.all_gather(grad_out, "fsdp", axis=0, tiled=True),
    )
    gate_part = jnp.dot(inputs, gate_weight, preferred_element_type=jnp.float32)
    up_part = jnp.dot(inputs, up_weight, preferred_element_type=jnp.float32)
    back_part = contract(cotangent, down_weight, 1, 1)
    gate, up_value, grad_hidden = lax.psum((gate_part, up_part, back_part), "tp")
    hidden, grad_gate_pre, grad_up_pre = swiglu_back(gate, up_value, grad_hidden)
    grad_gate = contract(inputs, grad_gate_pre, 0, 0).astype(jnp.bfloat16)
    grad_up = contract(inputs, grad_up_pre, 0, 0).astype(jnp.bfloat16)
    grad_down = contract(hidden, cotangent, 0, 0).astype(jnp.bfloat16)
    grad_tokens = lax.psum_scatter(
        contract(grad_gate_pre, gate_weight, 1, 1) + contract(grad_up_pre, up_weight, 1, 1),
        "fsdp",
        scatter_dimension=0,
        tiled=True,
    ).astype(jnp.bfloat16)
    return (grad_tokens, grad_gate, grad_up, grad_down)


def solution(mesh):
    return jax.shard_map(
        local,
        mesh=mesh,
        in_specs=(
            P("fsdp", "tp"),
            P("fsdp", "tp"),
            P("tp", "fsdp"),
            P("tp", "fsdp"),
            P("tp", "fsdp"),
            P("tp", "fsdp"),
            P("fsdp", "tp"),
            P("fsdp", "tp"),
        ),
        out_specs=(P("fsdp", "tp"), P("tp", "fsdp"), P("tp", "fsdp"), P("fsdp", "tp")),
        check_vma=False,
    )
```

profile of v0, /device:TPU:32, one launch (start us, length us, event | category | flops | bytes accessed | tf_op | source)
XLA Modules:
  0.0 1436.5 jit_solution(1583797035950069250)
XLA Ops:
  7.2 0.0 all-reduce.5.cloned.1.call-start
  7.2 338.4 %all-gather.1 = bf16[96,3,1024]{2,1,0:T(4,128)(2,1)S(1)} all-gather(bf16[1,3,1024]{2,1,0:T(4,128)(2,1)} %bitcast.55), channel_id=1, replica_groups=mesh['fsdp'=96,'tp'=8] {'fsdp'}, dimensions={0}, use_global_device_ids=true | all-gather | bytes 595968 | tf_op jit(solution)/shard_map/all_gather | solution.py:40
  345.6 0.5 reshape.23
  346.1 1.2 copy.21
  347.3 322.8 %all-gather = bf16[96,3,1024]{2,1,0:T(4,128)(2,1)S(1)} all-gather(bf16[1,3,1024]{2,1,0:T(4,128)(2,1)S(1)} %bitcast.56), channel_id=1, replica_groups=mesh['fsdp'=96,'tp'=8] {'fsdp'}, dimensions={0}, use_global_device_ids=true | all-gather | bytes 595968 | tf_op jit(solution)/shard_map/all_gather | solution.py:41
  670.1 0.5 reshape.21
  670.6 0.3 copy.20
  671.0 0.0 copy-start.2
  671.0 0.2 mul.61
  671.1 0.9 copy-done.2
  672.1 1.3 convolution_bitcast_fusion
  673.4 0.2 mul.57
  673.6 0.0 copy-start.13
  673.6 1.3 convolution_bitcast_fusion.1
  674.9 0.2 mul.54
  675.1 1.0 copy-done.7
  676.1 1.3 convolution_bitcast_fusion.2
  677.4 0.0 all-reduce.5.cloned.1.call-update
  677.4 1.3 dynamic-slice
  679.3 81.1 %all-reduce.5.cloned.1.call-done = (f32[288,384]{1,0:T(8,128)}, f32[288,384]{1,0:T(8,128)}, f32[288,384]{1,0:T(8,128)}) async-done(((f32[288,384]{1,0:T(8,128)}, f32[288,384]{1,0:T(8,128)}, f32[288,384]{1,0:T(8,128)}), (f32[288,384]{1,0:T(8,128)}, f32[288,384]{1,0:T(8,128)}, f32[288,384]{1,0:T(8,128)})) %all-reduce.5.cloned.1.call-update) | async-done | bytes 1327120 | tf_op jit(solution)/shard_map/psum | solution.py:46
  760.4 1.6 multiply_convert_fusion.1
  762.0 0.5 fusion.11
  762.6 0.6 fusion.3
  763.2 0.4 copy-done.8
  763.6 0.1 copy-done.9
  763.7 1.5 convolution_convert_fusion
  765.2 1.5 fusion.4
  766.7 0.5 convolution_add_fusion
  767.2 659.5 %all-reduce.6 = bf16[288,1024]{1,0:T(8,128)(2,1)S(1)} all-reduce(f32[288,1024]{1,0:T(8,128)S(1)} %convolution_add_fusion), channel_id=2, replica_groups=mesh['fsdp'=96,'tp'=8] {'fsdp'}, use_global_device_ids=true, to_apply=%region_3.0.clone | all-reduce | flops 294912 | bytes 1769472
  1426.8 1.2 copy.22
  1427.9 1.2 copy.23
  1429.1 0.6 dynamic-slice_convert_fusion
  (22 shorter events, 0.0 us)
Async XLA Ops:
  7.2 339.0 %copy-start.5 = (bf16[1024,384]{1,0:T(8,128)(2,1)S(1)}, bf16[1024,384]{1,0:T(8,128)(2,1)}, u32[]{:S(2)}) copy-start(bf16[1024,384]{1,0:T(8,128)(2,1)} %param.10) | copy-start | bytes 2359300
  7.2 753.2 %all-reduce.5.cloned.1.call-start = ((), (), s32[]{:S(2)}) async-start(), calls=%async_computation | async-start | bytes 2654208 | tf_op jit(solution)/shard_map/psum | solution.py:46
  345.6 1.7 copy-start.10
  347.3 323.3 %copy-start.6 = (bf16[1024,384]{1,0:T(8,128)(2,1)S(1)}, bf16[1024,384]{1,0:T(8,128)(2,1)}, u32[]{:S(2)}) copy-start(bf16[1024,384]{1,0:T(8,128)(2,1)} %param.12) | copy-start | bytes 2359300
  670.1 0.8 copy-start.11
  671.0 1.1 copy-start.2
  672.1 1.3 copy-start.12
  673.6 1.3 copy-start
  673.6 1.3 copy-start.13
  674.9 1.1 copy-start.7
  760.4 1.6 copy-start.3
  762.5 1.0 copy-start.8
  762.6 1.1 copy-start.9
  765.2 1.5 copy-start.1
  767.2 660.7 %copy-start.4 = (bf16[1024,384]{0,1:T(8,128)(2,1)S(1)}, bf16[1024,384]{0,1:T(8,128)(2,1)}, u32[]{:S(2)}) copy-start(bf16[1024,384]{0,1:T(8,128)(2,1)} %fusion.4) | copy-start | bytes 2359300
Sparse Core Ops, SparseCore 0:
  677.5 82.8 all-reduce.4
where the time goes:
time: 1440 us
  blocking collectives  1320 us (92%)
  waiting for transfers between devices  81.1 us (6%)
  between operations  14.9 us (1%)
    unnamed x1, blocking collectives  660 us
    all_gather x1, blocking collectives, local(): lax.all_gather(tokens, 'fsdp', axis=0, tiled=True)  338 us
    all_gather x1, blocking collectives, local(): lax.all_gather(grad_out, 'fsdp', axis=0, tiled=True)  323 us
    psum x1, waiting for transfers between devices, local(): lax.psum((gate_part, up_part, back_part), 'tp')  81.1 us
  transfers between devices with their start and end apart: 1, of which 1 were waited for; matrix products, arithmetic and copies ran while one was open for 0% of the time, Pallas kernels for 0%

commit v1 on v0

v1 whole, which is shorter than its diff:
```python
import functools

import jax
import jax.numpy as jnp
from jax import lax
from jax.experimental import pallas as pl
from jax.experimental.pallas import tpu as pltpu
from jax.sharding import PartitionSpec as P

BF = jnp.bfloat16
F32 = jnp.float32
NY, NX, NZH, NZ = 8, 4, 3, 4
TOK, FEAT, HID = 288, 1024, 384
SEG = 112
HALF = NZ * SEG
MESH = pl.DeviceIdType.MESH

_IDS = {}


def _id(*key):
    return _IDS.setdefault(key, len(_IDS))


for _a in range(2):
    for _d in (1, 2):
        _id("gz", _a, _d)
    for _d in range(1, NY):
        _id("gy", _a, _d)
    for _k in ("gxr", "gxl", "gxr2", "gxl2"):
        _id(_k, _a)
for _k in range(3):
    _id("core", _k)
    for _d in range(1, NZ):
        _id("z", _k, _d)
for _k in range(2):
    for _d in range(NZ):
        _id("back", _k, _d)
        _id("backcore", _k, _d)
for _k in ("x2r", "x2l", "x1r", "x1l", "xcr", "xcl"):
    _id(_k)
for _d in range(1, NY):
    _id("sy", _d)
for _d in (1, 2):
    _id("sz", _d)
N_IDS = len(_IDS)


def nt(left, right):
    return lax.dot_general(left, right, (((1,), (1,)), ((), ())), preferred_element_type=F32)


def tn(left, right):
    return lax.dot_general(left, right, (((0,), (0,)), ((), ())), preferred_element_type=F32)


def kernel(
    tok, gout, gc, gs, uc, us, dc, dsc,
    gt, gg, gu, gd,
    wg, wu, wd, G, st, X, U, RA, S, RB, HH, T, TB, RX1, RX2, RXa, RXb, CA, CB,
    YB, YF, RY, ZB, RZ, og, ou, od, fin,
    lsem, ssem, rsem,
):
    f = lax.axis_index("fsdp")
    tp = lax.axis_index("tp")
    y, zh, x = f // 12, lax.rem(f // 4, 3), lax.rem(f, 4)
    z, core = tp // 2, lax.rem(tp, 2)

    def dev(y=y, zh=zh, x=x, z=z, core=core):
        return ((y * 3 + zh) * 4 + x, z * 2 + core)

    def wrap(v, n):
        return lax.rem(v + n, n)

    def up(v, d, n):
        return lax.rem(v + d, n)

    def rcopy(key, src, dst, to):
        i = _IDS[key]
        return pltpu.make_async_remote_copy(
            src_ref=src, dst_ref=dst, send_sem=ssem.at[i], recv_sem=rsem.at[i],
            device_id=to, device_id_type=MESH,
        )

    sent = []

    def send(key, src, dst, to):
        c = rcopy(key, src, dst, to)
        c.start()
        sent.append(c)

    def recv(key, dst):
        rcopy(key, dst, dst, dev(core=1 - core)).wait_recv()

    loads = [
        pltpu.make_async_copy(s, d, lsem.at[i])
        for i, (s, d) in enumerate(((gc, wg), (uc, wu), (dc, wd)))
    ]
    for c in loads:
        c.start()

    barrier = pltpu.get_barrier_semaphore()
    partners = (
        [dev(zh=up(zh, d, 3)) for d in (1, 2)]
        + [dev(y=up(y, d, NY)) for d in range(1, NY)]
        + [dev(x=up(x, d, NX)) for d in (1, 3)]
        + [dev(z=up(z, d, NZ)) for d in range(1, NZ)]
        + [dev(core=1 - core)]
    )
    for p in partners:
        pl.semaphore_signal(barrier, inc=1, device_id=p, device_id_type=MESH)

    for a, ref in ((0, tok), (1, gout)):
        v = ref[...].astype(F32)
        for r in range(3):
            for c in range(8):
                st[a * 24 + r * 8 + c : a * 24 + r * 8 + c + 1, :] = v[r : r + 1, c * 128 : (c + 1) * 128]
        G[a, y, x, zh] = st[a * 24 : (a + 1) * 24, :].astype(BF)

    pl.semaphore_wait(barrier, len(partners))

    for a in range(2):
        for d in (1, 2):
            blk = G.at[a, y, x, zh]
            send(("gz", a, d), blk, blk, dev(zh=up(zh, d, 3)))

    def dequant(i, w, sc):
        loads[i].wait()
        nr, nc = w.shape[0] // 128, w.shape[1] // 128
        for r in range(nr):
            for c in range(nc):
                t = w[r * 128 : (r + 1) * 128, c * 128 : (c + 1) * 128]
                w[r * 128 : (r + 1) * 128, c * 128 : (c + 1) * 128] = (t.astype(F32) * sc[r, c]).astype(BF)

    dequant(0, wg, gs)
    for a in range(2):
        for d in (1, 2):
            recv(("gz", a, d), G.at[a, y, x, wrap(zh - d, 3)])
        for d in range(1, NY):
            send(("gy", a, d), G.at[a, y, x], G.at[a, y, x], dev(y=up(y, d, NY)))
    dequant(1, wu, us)
    dequant(2, wd, dsc)
    right, left = dev(x=up(x, 1, NX)), dev(x=up(x, 3, NX))
    xr, xl, xo = up(x, 1, NX), up(x, 3, NX), up(x, 2, NX)
    for a in range(2):
        for d in range(1, NY):
            recv(("gy", a, d), G.at[a, wrap(y - d, NY), x])
        send(("gxr", a), G.at[a, :, x], G.at[a, :, x], right)
        send(("gxl", a), G.at[a, :, x], G.at[a, :, x], left)

    def forward(a):
        recv(("gxr", a), G.at[a, :, xl])
        send(("gxr2", a), G.at[a, 0:4, xl], G.at[a, 0:4, xl], right)
        recv(("gxl", a), G.at[a, :, xr])
        send(("gxl2", a), G.at[a, 4:8, xr], G.at[a, 4:8, xr], left)

    def unpack(a):
        recv(("gxr2", a), G.at[a, 0:4, xo])
        recv(("gxl2", a), G.at[a, 4:8, xo])

        @pl.loop(0, NY)
        def _(yy):
            for xx in range(NX):
                for zz in range(NZH):
                    row = pl.multiple_of((yy * 12 + xx * 3 + zz) * 24, 8)
                    st[pl.ds(row, 24), :] = G[a, yy, xx, zz].astype(F32)

        for c in range(8):
            X[a, :, c * 128 : (c + 1) * 128] = st[pl.ds(c, TOK, stride=8), :].astype(BF)

    other = dev(core=1 - core)
    mine = pl.multiple_of(core * HALF, 16)
    theirs = pl.multiple_of((1 - core) * HALF, 16)

    def put(k, part):
        for j in range(3):
            U[k, j * TOK : (j + 1) * TOK, :] = part[:, j * 128 : (j + 1) * 128].astype(BF)
        U[k, 3 * TOK :, :] = jnp.zeros((2 * HALF - 3 * TOK, 128), BF)
        send(("core", k), U.at[k, pl.ds(theirs, HALF)], RA.at[k], other)

    def chip_sum(k):
        recv(("core", k), RA.at[k])
        S[k] = (U[k, pl.ds(mine, HALF), :].astype(F32) + RA[k].astype(F32)).astype(BF)
        for d in range(1, NZ):
            zz = up(z, d, NZ)
            send(("z", k, d), S.at[k, pl.ds(pl.multiple_of(zz * SEG, 16), SEG)], RB.at[d - 1, k], dev(z=zz))

    forward(0)
    unpack(0)
    put(0, jnp.dot(X[0], wg[...], preferred_element_type=F32))
    put(1, jnp.dot(X[0], wu[...], preferred_element_type=F32))
    forward(1)
    chip_sum(0)
    chip_sum(1)
    unpack(1)
    put(2, nt(X[1], wd[...]))
    chip_sum(2)

    own = pl.multiple_of(z * SEG, 16)

    def total(k):
        t = S[k, pl.ds(own, SEG), :].astype(F32)
        for d in range(1, NZ):
            recv(("z", k, d), RB.at[d - 1, k])
            t = t + RB[d - 1, k].astype(F32)
        return t

    gate = total(0)
    up_value = total(1)
    grad_hidden = total(2)
    sig = jax.nn.sigmoid(gate)
    act = gate * sig
    at = pl.ds(pl.multiple_of(core * HALF + z * SEG, 16), SEG)
    HH[0, at, :] = (grad_hidden * up_value * sig * (1.0 + gate * (1.0 - sig))).astype(BF)
    HH[1, at, :] = (grad_hidden * act).astype(BF)
    HH[2, at, :] = (act * up_value).astype(BF)

    groups = ((0, 2), (2, 1))
    for k, (lo, n) in enumerate(groups):
        seg = HH.at[pl.ds(lo, n), at]
        for d in range(1, NZ):
            send(("back", k, d), seg, seg, dev(z=up(z, d, NZ)))
        send(("backcore", k, 0), seg, seg, other)

    def spread(k):
        lo, n = groups[k]
        for d in range(1, NZ):
            zz = wrap(z - d, NZ)
            seg = HH.at[pl.ds(lo, n), pl.ds(pl.multiple_of(core * HALF + zz * SEG, 16), SEG)]
            recv(("back", k, d), seg)
            send(("backcore", k, d), seg, seg, other)

    def collect(k):
        lo, n = groups[k]
        for d in range(NZ):
            zz = wrap(z - d, NZ)
            recv(("backcore", k, d), HH.at[pl.ds(lo, n), pl.ds(pl.multiple_of((1 - core) * HALF + zz * SEG, 16), SEG)])

    def whole(k):
        return jnp.concatenate([HH[k, j * TOK : (j + 1) * TOK, :] for j in range(3)], axis=1)

    spread(0)
    collect(0)
    ggp, gup = whole(0), whole(1)
    for n in range(4):
        rows = slice(n * 256, (n + 1) * 256)
        part = nt(ggp, wg[rows, :]) + nt(gup, wu[rows, :])
        for h in range(2):
            T[pl.ds(n * 2 + h, TOK, stride=8), :] = part[:, h * 128 : (h + 1) * 128]

    @pl.loop(0, NY)
    def _(yy):
        for xx in range(NX):
            TB[xx, yy] = T[pl.ds(pl.multiple_of((yy * 4 + xx) * 72, 8), 72), :].astype(BF)

    send(("x2r",), TB.at[xo, 0:4], RXa, right)
    send(("x2l",), TB.at[xo, 4:8], RXb, left)
    send(("x1r",), TB.at[xr, 4:8], RX1.at[4:8], right)
    send(("x1l",), TB.at[xl, 0:4], RX2.at[0:4], left)

    spread(1)

    def mine_of(yy, xx):
        return T[pl.ds(pl.multiple_of((yy * 4 + xx) * 72, 8), 72), :]

    recv(("x2r",), RXa)
    for i in range(4):
        CA[i] = (mine_of(i, xr) + RXa[i].astype(F32)).astype(BF)
    send(("xcr",), CA, RX1.at[0:4], right)
    recv(("x2l",), RXb)
    for i in range(4):
        CB[i] = (mine_of(4 + i, xl) + RXb[i].astype(F32)).astype(BF)
    send(("xcl",), CB, RX2.at[4:8], left)

    both = jnp.concatenate([ggp, gup], axis=1)
    stores = []

    def store(src, dst):
        c = pltpu.make_async_copy(src, dst, lsem.at[3 + len(stores)])
        c.start()
        stores.append(c)

    for n in range(4):
        rows = slice(n * 256, (n + 1) * 256)
        part = tn(X[0, :, rows], both)
        og[rows, :] = part[:, :HID].astype(BF)
        ou[rows, :] = part[:, HID:].astype(BF)
    store(og, gg)
    store(ou, gu)

    recv(("x1r",), RX1.at[4:8])
    recv(("x1l",), RX2.at[0:4])
    recv(("xcr",), RX1.at[0:4])
    recv(("xcl",), RX2.at[4:8])
    for i in range(NY):
        v = mine_of(i, x) + RX1[i].astype(F32) + RX2[i].astype(F32)
        YF[i] = v
        YB[i] = v.astype(BF)
    for d in range(1, NY):
        yy = up(y, d, NY)
        send(("sy", d), YB.at[yy], RY.at[d - 1], dev(y=yy))

    collect(1)
    hid = whole(2)
    for n in range(3):
        rows = slice(n * 128, (n + 1) * 128)
        od[rows, :] = tn(hid[:, rows], X[1]).astype(BF)
    store(od, gd)

    v = YF[y]
    for d in range(1, NY):
        recv(("sy", d), RY.at[d - 1])
        v = v + RY[d - 1].astype(F32)
    for i in range(NZH):
        ZB[i] = v[i * 24 : (i + 1) * 24, :]
    for d in (1, 2):
        zz = up(zh, d, 3)
        send(("sz", d), ZB.at[zz], RZ.at[d - 1], dev(zh=zz))
    v = ZB[zh]
    for d in (1, 2):
        recv(("sz", d), RZ.at[d - 1])
        v = v + RZ[d - 1]
    for r in range(3):
        for c in range(8):
            fin[r : r + 1, c * 128 : (c + 1) * 128] = v[r * 8 + c : r * 8 + c + 1, :]
    gt[...] = fin[0:3, :].astype(BF)

    for c in stores:
        c.wait()
    for c in sent:
        c.wait_send()


def local(*args):
    vmem = pl.BlockSpec(memory_space=pltpu.VMEM)
    smem = pl.BlockSpec(memory_space=pltpu.SMEM)
    hbm = pl.BlockSpec(memory_space=pl.ANY)
    V = pltpu.VMEM
    return pl.pallas_call(
        kernel,
        out_shape=(
            jax.ShapeDtypeStruct((3, FEAT), BF),
            jax.ShapeDtypeStruct((FEAT, HID), BF),
            jax.ShapeDtypeStruct((FEAT, HID), BF),
            jax.ShapeDtypeStruct((HID, FEAT), BF),
        ),
        in_specs=[vmem, vmem, hbm, smem, hbm, smem, hbm, smem],
        out_specs=(vmem, hbm, hbm, hbm),
        scratch_shapes=[
            V((FEAT, HID), BF), V((FEAT, HID), BF), V((HID, FEAT), BF),
            V((2, NY, NX, NZH, 24, 128), BF),
            V((TOK * 8, 128), F32),
            V((2, TOK, FEAT), BF),
            V((3, 2 * HALF, 128), BF),
            V((3, HALF, 128), BF),
            V((3, HALF, 128), BF),
            V((3, 3, SEG, 128), BF),
            V((3, 2 * HALF, 128), BF),
            V((TOK * 8, 128), F32),
            V((NX, NY, 72, 128), BF),
            V((NY, 72, 128), BF), V((NY, 72, 128), BF),
            V((4, 72, 128), BF), V((4, 72, 128), BF),
            V((4, 72, 128), BF), V((4, 72, 128), BF),
            V((NY, 72, 128), BF), V((NY, 72, 128), F32), V((NY - 1, 72, 128), BF),
            V((NZH, 24, 128), F32), V((2, 24, 128), F32),
            V((FEAT, HID), BF), V((FEAT, HID), BF), V((HID, FEAT), BF),
            V((8, FEAT), F32),
            pltpu.SemaphoreType.DMA((6,)),
            pltpu.SemaphoreType.DMA((N_IDS,)),
            pltpu.SemaphoreType.DMA((N_IDS,)),
        ],
        compiler_params=pltpu.CompilerParams(
            collective_id=0, has_side_effects=True, vmem_limit_bytes=48 * 1024 * 1024
        ),
    )(*args)


def solution(mesh):
    return jax.shard_map(
        local,
        mesh=mesh,
        in_specs=(
            P("fsdp", "tp"),
            P("fsdp", "tp"),
            P("tp", "fsdp"),
            P("tp", "fsdp"),
            P("tp", "fsdp"),
            P("tp", "fsdp"),
            P("fsdp", "tp"),
            P("fsdp", "tp"),
        ),
        out_specs=(P("fsdp", "tp"), P("tp", "fsdp"), P("tp", "fsdp"), P("fsdp", "tp")),
        check_vma=False,
    )
```

time: 1440 us -> 90 us (0.06)
  the two profiles are of different devices: /device:TPU:32 before, /device:TPU:2 now
where the time goes in v1:
time: 90 us; the launch traced here: 89.6 us
  Pallas kernels  80.1 us (89%)
  local copies, waits for them, and re-layouts  8.79 us (10%)
    pallas_call x1, Pallas kernels, local(): pl.pallas_call(kernel, out_shape=(jax.ShapeDtypeStruct((3, FEAT), BF), ja...  80.1 us
    unnamed x20, local copies, waits for them, and re-layouts  8.79 us

profile of v1, /device:TPU:2, one launch (start us, length us, event | category | flops | bytes accessed | tf_op | source)
XLA Modules:
  0.0 89.6 jit_solution(14377250220217278882)
XLA Ops:
  0.6 0.0 copy-start.6
  0.6 0.0 copy-start.3
  0.7 0.8 copy.12.gs
  1.4 0.0 copy-done.6
  1.4 0.0 copy-start.5
  1.4 0.1 copy.13.us
  1.5 0.0 copy-done.3
  1.5 0.6 copy-done.5
  2.1 0.0 copy-start
  2.1 1.1 %copy-done = bf16[1024,384]{1,0:T(8,128)(2,1)S(1)} copy-done((bf16[1024,384]{1,0:T(8,128)(2,1)S(1)}, bf16[1024,384]{1,0:T(8,128)(2,1)}, u32[]{:S(2)}) %copy-start) | copy-done | bytes 786456
  3.2 0.0 copy-start.1
  3.2 1.1 %copy-done.1 = bf16[1024,384]{1,0:T(8,128)(2,1)S(1)} copy-done((bf16[1024,384]{1,0:T(8,128)(2,1)S(1)}, bf16[1024,384]{1,0:T(8,128)(2,1)}, u32[]{:S(2)}) %copy-start.1) | copy-done | bytes 786456
  4.4 0.0 copy-start.2
  4.4 1.1 %copy-done.2 = bf16[384,1024]{1,0:T(8,128)(2,1)S(1)} copy-done((bf16[384,1024]{1,0:T(8,128)(2,1)S(1)}, bf16[384,1024]{1,0:T(8,128)(2,1)}, u32[]{:S(2)}) %copy-start.2) | copy-done | bytes 786456
  5.5 0.0 copy-start.4
  5.5 0.7 copy-done.4
  6.2 80.1 %shard_map.111 = (bf16[3,1024]{1,0:T(4,128)(2,1)S(1)}, bf16[1024,384]{1,0:T(8,128)(2,1)S(1)}, bf16[1024,384]{1,0:T(8,128)(2,1)S(1)}, bf16[384,1024]{1,0:T(8,128)(2,1)S(1)}) custom-call(bf16[3,1024]{1,0:T(4,128)(2,1)S(1)} %copy-done.3, bf16[3,1024]{1,0:T(4,128)(2,1)S(1)} %copy-done.4, bf16[1024,384]{1,0:T(8,128)(2,1)S(1)} %copy-done, f32[8,3]{1,0:T(8,128)S(1)} %copy.12.gs, ...), custom_call_target="tpu_custom_call" | custom-call | tf_op jit(solution)/shard_map/pallas_call | solution.py:339
  86.3 0.6 copy.18
  86.9 0.9 copy.19
  87.8 0.9 copy.20
  88.7 0.9 copy.21
Async XLA Ops:
  0.6 0.8 copy-start.6
  0.6 0.9 copy-start.3
  1.4 0.7 copy-start.5
  2.1 1.1 %copy-start = (bf16[1024,384]{1,0:T(8,128)(2,1)S(1)}, bf16[1024,384]{1,0:T(8,128)(2,1)}, u32[]{:S(2)}) copy-start(bf16[1024,384]{1,0:T(8,128)(2,1)} %gc.1) | copy-start | bytes 2359300
  3.2 1.1 %copy-start.1 = (bf16[1024,384]{1,0:T(8,128)(2,1)S(1)}, bf16[1024,384]{1,0:T(8,128)(2,1)}, u32[]{:S(2)}) copy-start(bf16[1024,384]{1,0:T(8,128)(2,1)} %uc.1) | copy-start | bytes 2359300
  4.4 1.1 %copy-start.2 = (bf16[384,1024]{1,0:T(8,128)(2,1)S(1)}, bf16[384,1024]{1,0:T(8,128)(2,1)}, u32[]{:S(2)}) copy-start(bf16[384,1024]{1,0:T(8,128)(2,1)} %dc.1) | copy-start | bytes 2359300
  5.5 0.7 copy-start.4

commit v2 on v0

v2 whole, which is shorter than its diff:
```python
import functools

import jax
import jax.numpy as jnp
from jax import lax
from jax.experimental import pallas as pl
from jax.experimental.pallas import tpu as pltpu
from jax.sharding import PartitionSpec as P

BF = jnp.bfloat16
F32 = jnp.float32
NY, NX, NZH, NZ = 8, 4, 3, 4
TOK, FEAT, HID = 288, 1024, 384
MESH = pl.DeviceIdType.MESH

NB = (1, 2)
NT = (96, 192)
FIRST = (0, 96)
SEG = (48, 80)
HALF = (192, 320)

_IDS = {}


def _id(*key):
    return _IDS.setdefault(key, len(_IDS))


for _d in (1, 2):
    _id("gz", _d)
    _id("sz", _d)
for _h in range(2):
    for _d in range(1, NY):
        _id("gy", _h, _d)
        _id("sy", _h, _d)
    for _k in ("gxr", "gxl", "gxr2", "gxl2", "core", "x2r", "x2l", "x1r", "x1l", "xcr", "xcl"):
        _id(_k, _h)
    for _d in range(1, NZ):
        _id("z", _h, _d)
for _k in range(3):
    for _d in range(NZ):
        _id("back", _k, _d)
        _id("backcore", _k, _d)
N_IDS = len(_IDS)


def nt(left, right):
    return lax.dot_general(left, right, (((1,), (1,)), ((), ())), preferred_element_type=F32)


def tn(left, right):
    return lax.dot_general(left, right, (((0,), (0,)), ((), ())), preferred_element_type=F32)


def kernel(
    tok_in, gout_in, gc, gs_in, uc, us_in, dc, ds_in,
    gt, gg, gu, gd,
    tok, gout, gs, us, dsc, wg, wu, wd, X, og, ou, od, fin, ZB, RZ,
    *rest,
):
    per, (lsem, ssem, rsem) = (rest[:19], rest[19:38]), rest[38:]
    G, st, U, UB, RA, S, RB, HH, T, TB, RX1, RX2, RXa, RXb, CA, CB, YB, YF, RY = zip(*per)

    f = lax.axis_index("fsdp")
    tp = lax.axis_index("tp")
    y, zh, x = f // 12, lax.rem(f // 4, 3), lax.rem(f, 4)
    z, core = tp // 2, lax.rem(tp, 2)

    def dev(y=y, zh=zh, x=x, z=z, core=core):
        return ((y * 3 + zh) * 4 + x, z * 2 + core)

    def up(v, d, n):
        return lax.rem(v + n + d, n)

    def rcopy(key, src, dst, to):
        i = _IDS[key]
        return pltpu.make_async_remote_copy(
            src_ref=src, dst_ref=dst, send_sem=ssem.at[i], recv_sem=rsem.at[i],
            device_id=to, device_id_type=MESH,
        )

    sent = []

    def send(key, src, dst, to):
        c = rcopy(key, src, dst, to)
        c.start()
        sent.append(c)

    def recv(key, dst):
        rcopy(key, dst, dst, dev(core=1 - core)).wait_recv()

    barrier = pltpu.get_barrier_semaphore()
    partners = (
        [dev(y=up(y, d, NY)) for d in range(1, NY)]
        + [dev(zh=up(zh, d, 3)) for d in (1, 2)]
        + [dev(x=up(x, d, NX)) for d in (1, 3)]
        + [dev(z=up(z, d, NZ)) for d in range(1, NZ)]
        + [dev(core=1 - core)]
    )
    for p in partners:
        pl.semaphore_signal(barrier, inc=1, device_id=p, device_id_type=MESH)

    loads = [
        pltpu.make_async_copy(s, d, lsem.at[i])
        for i, (s, d) in enumerate((
            (gc, wg), (uc, wu), (dc, wd), (tok_in, tok), (gout_in, gout), (gs_in, gs), (us_in, us), (ds_in, dsc),
        ))
    ]
    for i in (3, 4, 5, 0, 6, 1, 7, 2):
        loads[i].start()

    for a, ref in ((0, tok), (1, gout)):
        loads[3 + a].wait()
        v = ref[...].astype(F32)
        for r in range(3):
            for c in range(8):
                st[0][a * 24 + r * 8 + c : a * 24 + r * 8 + c + 1, :] = v[r : r + 1, c * 128 : (c + 1) * 128]
        G[0][0, 0, 0, a] = st[0][a * 24 : (a + 1) * 24, :].astype(BF)

    pl.semaphore_wait(barrier, len(partners))

    def spread_y(h):
        for d in (4, 3, 5, 2, 6, 1, 7):
            send(("gy", h, d), G[h].at[0, 0], G[h].at[0, d], dev(y=up(y, d, NY)))

    right, left = dev(x=up(x, 1, NX)), dev(x=up(x, 3, NX))
    other = dev(core=1 - core)

    def spread_x(h):
        for d in range(1, NY):
            recv(("gy", h, d), G[h].at[0, d])
        send(("gxr", h), G[h].at[0], G[h].at[1], right)
        send(("gxl", h), G[h].at[0], G[h].at[2], left)

    def forward(h):
        recv(("gxr", h), G[h].at[1])
        send(("gxr2", h), G[h].at[1, 0:4], G[h].at[3, 0:4], right)
        recv(("gxl", h), G[h].at[2])
        send(("gxl2", h), G[h].at[2, 4:8], G[h].at[3, 4:8], left)

    def gathered(h):
        recv(("gxr2", h), G[h].at[3, 0:4])
        recv(("gxl2", h), G[h].at[3, 4:8])

    def dequant(i, w, sc):
        loads[i].wait()
        loads[5 + i].wait()
        nr, nc = w.shape[0] // 128, w.shape[1] // 128
        for r in range(nr):
            for c in range(nc):
                t = w[r * 128 : (r + 1) * 128, c * 128 : (c + 1) * 128]
                w[r * 128 : (r + 1) * 128, c * 128 : (c + 1) * 128] = (t.astype(F32) * (sc[c, r] if i < 2 else sc[r, c])).astype(BF)

    def tokens_of(h):
        return slice(FIRST[h], FIRST[h] + NT[h])

    def unpack(h, a):
        n = 192 * NB[h]
        for slot in range(NX):
            for k in range(NB[h]):
                for d in range(NY):
                    row = slot * n + (d * NB[h] + k) * 24
                    st[h][row : row + 24, :] = G[h][slot, d, k, a].astype(F32)
        for c in range(8):
            X[a, tokens_of(h), c * 128 : (c + 1) * 128] = st[h][pl.ds(c, NT[h], stride=8), :].astype(BF)

    def put(h, k, part):
        for j in range(3):
            U[h][k, j * NT[h] : (j + 1) * NT[h], :] = part[:, j * 128 : (j + 1) * 128]

    def rows(start, n):
        return pl.ds(pl.multiple_of(start, 16), n)

    def hand(h):
        unpack(h, 0)
        put(h, 0, jnp.dot(X[0, tokens_of(h), :], wg[...], preferred_element_type=F32))
        put(h, 1, jnp.dot(X[0, tokens_of(h), :], wu[...], preferred_element_type=F32))
        unpack(h, 1)
        put(h, 2, nt(X[1, tokens_of(h), :], wd[...]))
        for k in range(3):
            UB[h][k] = U[h][k, rows((1 - core) * HALF[h], HALF[h]), :].astype(BF)
        send(("core", h), UB[h], RA[h], other)

    def chip_sum(h):
        recv(("core", h), RA[h])
        for k in range(3):
            S[h][k] = (U[h][k, rows(core * HALF[h], HALF[h]), :] + RA[h][k].astype(F32)).astype(BF)
        for d in (2, 1, 3):
            zz = up(z, d, NZ)
            send(("z", h, d), S[h].at[:, rows(zz * SEG[h], SEG[h])], RB[h].at[d - 1], dev(z=zz))

    def share(h, zz, cc):
        return rows(cc * HALF[h] + zz * SEG[h], SEG[h])

    def middle(h):
        for d in range(1, NZ):
            recv(("z", h, d), RB[h].at[d - 1])

        def total(k):
            t = U[h][k, share(h, z, core), :] + RA[h][k, rows(z * SEG[h], SEG[h]), :].astype(F32)
            for d in range(1, NZ):
                t = t + RB[h][d - 1, k].astype(F32)
            return t

        gate, up_value, grad_hidden = total(0), total(1), total(2)
        sig = jax.nn.sigmoid(gate)
        act = gate * sig
        at = share(h, z, core)
        HH[h][0, at, :] = (grad_hidden * up_value * sig * (1.0 + gate * (1.0 - sig))).astype(BF)
        HH[h][1, at, :] = (grad_hidden * act).astype(BF)
        HH[h][2, at, :] = (act * up_value).astype(BF)

    groups = ((0, 0, 3), (1, 0, 2), (1, 2, 1))

    def piece(g, zz, cc):
        h, lo, n = groups[g]
        return HH[h].at[pl.ds(lo, n), share(h, zz, cc)]

    def give(g):
        seg = piece(g, z, core)
        for d in (2, 1, 3):
            send(("back", g, d), seg, seg, dev(z=up(z, d, NZ)))
        send(("backcore", g, 0), seg, seg, other)

    def spread(g):
        for d in (1, 3, 2):
            seg = piece(g, up(z, -d, NZ), core)
            recv(("back", g, d), seg)
            send(("backcore", g, d), seg, seg, other)

    def collect(g):
        for d in range(NZ):
            recv(("backcore", g, d), piece(g, up(z, -d, NZ), 1 - core))

    def whole(h, k):
        return jnp.concatenate([HH[h][k, j * NT[h] : (j + 1) * NT[h], :] for j in range(3)], axis=1)

    def input_grad(h):
        ggp, gup = whole(h, 0), whole(h, 1)
        for n in range(4):
            r = slice(n * 256, (n + 1) * 256)
            part = nt(ggp, wg[r, :]) + nt(gup, wu[r, :])
            for q in range(2):
                T[h][pl.ds(n * 2 + q, NT[h], stride=8), :] = part[:, q * 128 : (q + 1) * 128]

    def slab(h, p, lo, hi):
        n = 24 * NB[h]
        return T[h][(p * 8 + lo) * n : (p * 8 + hi) * n, :].reshape(hi - lo, n, 128)

    def sum_x(h):
        TB[h][3] = slab(h, 3, 0, 8).astype(BF)
        send(("x2r", h), TB[h].at[3, 0:4], RXa[h], right)
        send(("x2l", h), TB[h].at[3, 4:8], RXb[h], left)
        TB[h][2, 4:8] = slab(h, 2, 4, 8).astype(BF)
        TB[h][1, 0:4] = slab(h, 1, 0, 4).astype(BF)
        send(("x1r", h), TB[h].at[2, 4:8], RX1[h].at[4:8], right)
        send(("x1l", h), TB[h].at[1, 0:4], RX2[h].at[0:4], left)

    def sum_x2(h):
        recv(("x2r", h), RXa[h])
        CA[h][...] = (slab(h, 2, 0, 4) + RXa[h][...].astype(F32)).astype(BF)
        send(("xcr", h), CA[h], RX1[h].at[0:4], right)
        recv(("x2l", h), RXb[h])
        CB[h][...] = (slab(h, 1, 4, 8) + RXb[h][...].astype(F32)).astype(BF)
        send(("xcl", h), CB[h], RX2[h].at[4:8], left)

    def sum_y(h):
        recv(("x1r", h), RX1[h].at[4:8])
        recv(("x1l", h), RX2[h].at[0:4])
        recv(("xcr", h), RX1[h].at[0:4])
        recv(("xcl", h), RX2[h].at[4:8])
        n = 24 * NB[h]
        for d in (4, 3, 5, 2, 6, 1, 7, 0):
            v = T[h][d * n : (d + 1) * n, :] + RX1[h][d].astype(F32) + RX2[h][d].astype(F32)
            if d:
                YB[h][d] = v.astype(BF)
                send(("sy", h, d), YB[h].at[d], RY[h].at[d - 1], dev(y=up(y, -d, NY)))
            else:
                YF[h][...] = v

    def summed_y(h):
        v = YF[h][...]
        for d in (1, 7, 2, 6, 3, 5, 4):
            recv(("sy", h, d), RY[h].at[d - 1])
            v = v + RY[h][d - 1].astype(F32)
        return v

    stores = []

    def store(src, dst):
        c = pltpu.make_async_copy(src, dst, lsem.at[8 + len(stores)])
        c.start()
        stores.append(c)

    for d in (1, 2):
        send(("gz", d), G[0].at[0, 0, 0], G[1].at[0, 0, d - 1], dev(zh=up(zh, d, 3)))
    spread_y(0)
    for h in range(2):
        for k in range(3):
            U[h][k, 3 * NT[h] :, :] = jnp.zeros((2 * HALF[h] - 3 * NT[h], 128), F32)
    dequant(0, wg, gs)
    dequant(1, wu, us)
    dequant(2, wd, dsc)
    for d in (1, 2):
        recv(("gz", d), G[1].at[0, 0, d - 1])
    spread_y(1)
    spread_x(0)
    forward(0)
    gathered(0)
    hand(0)
    spread_x(1)
    chip_sum(0)
    forward(1)
    middle(0)
    give(0)
    gathered(1)
    hand(1)
    spread(0)
    chip_sum(1)
    collect(0)
    input_grad(0)
    sum_x(0)
    sum_x2(0)
    middle(1)
    give(1)
    sum_y(0)
    spread(1)
    give(2)
    collect(1)
    input_grad(1)
    sum_x(1)
    own_sum = summed_y(0)
    fin[0:24, 0:128] = own_sum
    sum_x2(1)
    spread(2)

    both = jnp.concatenate(
        [jnp.concatenate([whole(h, 0), whole(h, 1)], axis=1) for h in range(2)], axis=0
    )

    def weight_grads(n):
        r = slice(n * 256, (n + 1) * 256)
        part = tn(X[0, :, r], both)
        og[r, :] = part[:, :HID].astype(BF)
        ou[r, :] = part[:, HID:].astype(BF)

    weight_grads(0)
    weight_grads(1)
    sum_y(1)
    weight_grads(2)
    weight_grads(3)
    store(og, gg)
    store(ou, gu)
    collect(2)
    hid = jnp.concatenate([whole(0, 2), whole(1, 2)], axis=0)
    for n in range(3):
        r = slice(n * 128, (n + 1) * 128)
        od[r, :] = tn(hid[:, r], X[1]).astype(BF)
    store(od, gd)

    v = summed_y(1)
    for i in range(2):
        ZB[i] = v[i * 24 : (i + 1) * 24, :]
    for d in (1, 2):
        send(("sz", d), ZB.at[d - 1], RZ.at[d - 1], dev(zh=up(zh, -d, 3)))
    v = fin[0:24, 0:128]
    for d in (1, 2):
        recv(("sz", d), RZ.at[d - 1])
        v = v + RZ[d - 1]
    for r in range(3):
        for c in range(8):
            fin[r : r + 1, c * 128 : (c + 1) * 128] = v[r * 8 + c : r * 8 + c + 1, :]
    gt[...] = fin[0:3, :].astype(BF)

    for c in stores:
        c.wait()
    for c in sent:
        c.wait_send()


def copies(*refs):
    ins, outs, bufs, isem, osem = refs[:4], refs[4:8], refs[8:12], refs[12], refs[13]
    parts = []
    for i in range(4):
        rows = ins[i].shape[0]
        n = 2 if i else 1
        parts += [(i, slice(j * rows // n, (j + 1) * rows // n)) for j in range(n)]
    loads = [pltpu.make_async_copy(ins[i].at[r], bufs[i].at[r], isem.at[k]) for k, (i, r) in enumerate(parts)]
    stores = [pltpu.make_async_copy(bufs[i].at[r], outs[i].at[r], osem.at[k]) for k, (i, r) in enumerate(parts)]
    for c in loads:
        c.start()
    for k, c in enumerate(loads):
        c.wait()
        stores[k].start()
    for c in stores:
        c.wait()


def chunk_scratch(h):
    V = pltpu.VMEM
    n, half, seg = 24 * NB[h], HALF[h], SEG[h]
    return [
        V((NX, NY, NB[h], 2, 24, 128), BF),
        V((NT[h] * 8, 128), F32),
        V((3, 2 * half, 128), F32),
        V((3, half, 128), BF), V((3, half, 128), BF), V((3, half, 128), BF),
        V((NZ - 1, 3, seg, 128), BF),
        V((3, 2 * half, 128), BF),
        V((NT[h] * 8, 128), F32),
        V((NX, NY, n, 128), BF),
        V((NY, n, 128), BF), V((NY, n, 128), BF),
        V((4, n, 128), BF), V((4, n, 128), BF), V((4, n, 128), BF), V((4, n, 128), BF),
        V((NY, n, 128), BF), V((n, 128), F32), V((NY - 1, n, 128), BF),
    ]


def local(tokens, grad_out, gate_codes, gate_scale, up_codes, up_scale, down_codes, down_scale):
    vmem = pl.BlockSpec(memory_space=pltpu.VMEM)
    hbm = pl.BlockSpec(memory_space=pl.ANY)
    V = pltpu.VMEM
    far = pl.BlockSpec(memory_space=pltpu.HBM)
    shapes = (
        jax.ShapeDtypeStruct((3, FEAT), BF),
        jax.ShapeDtypeStruct((FEAT, HID), BF),
        jax.ShapeDtypeStruct((FEAT, HID), BF),
        jax.ShapeDtypeStruct((HID, FEAT), BF),
    )
    results = pl.pallas_call(
        kernel,
        out_shape=shapes,
        in_specs=[far] * 8,
        out_specs=(vmem, hbm, hbm, hbm),
        scratch_shapes=[
            V((3, FEAT), BF), V((3, FEAT), BF),
            pltpu.SMEM((3, 8), F32), pltpu.SMEM((3, 8), F32), pltpu.SMEM((3, 8), F32),
            V((FEAT, HID), BF), V((FEAT, HID), BF), V((HID, FEAT), BF),
            V((2, TOK, FEAT), BF),
            V((FEAT, HID), BF), V((FEAT, HID), BF), V((HID, FEAT), BF),
            V((24, FEAT), F32),
            V((2, 24, 128), F32), V((2, 24, 128), F32),
            *chunk_scratch(0), *chunk_scratch(1),
            pltpu.SemaphoreType.DMA((11,)),
            pltpu.SemaphoreType.DMA((N_IDS,)),
            pltpu.SemaphoreType.DMA((N_IDS,)),
        ],
        compiler_params=pltpu.CompilerParams(
            collective_id=0, has_side_effects=True, vmem_limit_bytes=63 * 1024 * 1024
        ),
    )(tokens, grad_out, gate_codes, gate_scale.T, up_codes, up_scale.T, down_codes, down_scale)
    return pl.pallas_call(
        copies,
        out_shape=shapes,
        in_specs=[hbm] * 4,
        out_specs=(far,) * 4,
        scratch_shapes=[V(a.shape, BF) for a in shapes]
        + [pltpu.SemaphoreType.DMA((7,)), pltpu.SemaphoreType.DMA((7,))],
        compiler_params=pltpu.CompilerParams(vmem_limit_bytes=63 * 1024 * 1024),
    )(*results)


def solution(mesh):
    return jax.shard_map(
        local,
        mesh=mesh,
        in_specs=(
            P("fsdp", "tp"),
            P("fsdp", "tp"),
            P("tp", "fsdp"),
            P("tp", "fsdp"),
            P("tp", "fsdp"),
            P("tp", "fsdp"),
            P("fsdp", "tp"),
            P("fsdp", "tp"),
        ),
        out_specs=(P("fsdp", "tp"), P("tp", "fsdp"), P("tp", "fsdp"), P("fsdp", "tp")),
        check_vma=False,
    )
```

time: 1440 us -> 80.4 us (0.06)
  the two profiles are of different devices: /device:TPU:32 before, /device:TPU:2 now
where the time goes in v2:
time: 80.4 us; the launch traced here: 80.2 us
  Pallas kernels  79.5 us (99%)
    pallas_call x1, Pallas kernels, local(): pl.pallas_call(kernel, out_shape=shapes, in_specs=[far] * 8, out_specs=(v...  77 us
    pallas_call x1, Pallas kernels, local(): pl.pallas_call(copies, out_shape=shapes, in_specs=[hbm] * 4, out_specs=(f...  2.53 us

profile of v2, /device:TPU:2, one launch (start us, length us, event | category | flops | bytes accessed | tf_op | source)
XLA Modules:
  0.0 80.2 jit_solution(10103890451101631038)
XLA Ops:
  0.6 77.0 %shard_map.111 = (bf16[3,1024]{1,0:T(4,128)(2,1)}, bf16[1024,384]{1,0:T(8,128)(2,1)}, bf16[1024,384]{1,0:T(8,128)(2,1)}, bf16[384,1024]{1,0:T(8,128)(2,1)}) custom-call(bf16[3,1024]{1,0:T(4,128)(2,1)} %tok_in.1, bf16[3,1024]{1,0:T(4,128)(2,1)} %gout_in.1, bf16[1024,384]{1,0:T(8,128)(2,1)} %gc.1, f32[3,8]{1,0:T(4,128)} %bitcast.2, bf16[1024,384]{1,0:T(8,128)(2,1)} %uc.1, ...), custom_call_target="tpu_custom_call" | custom-call | tf_op jit(solution)/shard_map/pallas_call | solution.py:428
  77.6 2.5 %shard_map.112 = (bf16[3,1024]{1,0:T(4,128)(2,1)}, bf16[1024,384]{1,0:T(8,128)(2,1)}, bf16[1024,384]{1,0:T(8,128)(2,1)}, bf16[384,1024]{1,0:T(8,128)(2,1)}) custom-call(bf16[3,1024]{1,0:T(4,128)(2,1)} %get-tuple-element.8.refs_0_, bf16[1024,384]{1,0:T(8,128)(2,1)} %get-tuple-element.9.refs_1_, bf16[1024,384]{1,0:T(8,128)(2,1)} %get-tuple-element.10.refs_2_, ...), custom_call_target="tpu_custom_call" | custom-call | tf_op jit(solution)/shard_map/pallas_call | solution.py:450

commit v3 on v2

--- a/solution.py
+++ b/solution.py
@@ -33,7 +33,7 @@
     for _d in range(1, NY):
         _id("gy", _h, _d)
         _id("sy", _h, _d)
-    for _k in ("gxr", "gxl", "gxr2", "gxl2", "core", "x2r", "x2l", "x1r", "x1l", "xcr", "xcl"):
+    for _k in ("gxr", "gxl", "gxr2", "gxl2", "gxrb", "gxlb", "core", "x2r", "x2l", "x1r", "x1l", "xcr", "xcl"):
         _id(_k, _h)
     for _d in range(1, NZ):
         _id("z", _h, _d)
@@ -85,6 +85,11 @@
         c = rcopy(key, src, dst, to)
         c.start()
         sent.append(c)
+
+    def gone(n):
+        for c in sent[-n:]:
+            c.wait_send()
+        del sent[-n:]
 
     def recv(key, dst):
         rcopy(key, dst, dst, dev(core=1 - core)).wait_recv()
@@ -129,16 +134,22 @@
     def spread_x(h):
         for d in range(1, NY):
             recv(("gy", h, d), G[h].at[0, d])
-        send(("gxr", h), G[h].at[0], G[h].at[1], right)
-        send(("gxl", h), G[h].at[0], G[h].at[2], left)
+        send(("gxr", h), G[h].at[0, 0:4], G[h].at[1, 0:4], right)
+        send(("gxl", h), G[h].at[0, 4:8], G[h].at[2, 4:8], left)
+
+    def spread_x2(h):
+        send(("gxrb", h), G[h].at[0, 4:8], G[h].at[1, 4:8], right)
+        send(("gxlb", h), G[h].at[0, 0:4], G[h].at[2, 0:4], left)
 
     def forward(h):
-        recv(("gxr", h), G[h].at[1])
+        recv(("gxr", h), G[h].at[1, 0:4])
         send(("gxr2", h), G[h].at[1, 0:4], G[h].at[3, 0:4], right)
-        recv(("gxl", h), G[h].at[2])
+        recv(("gxl", h), G[h].at[2, 4:8])
         send(("gxl2", h), G[h].at[2, 4:8], G[h].at[3, 4:8], left)
 
     def gathered(h):
+        recv(("gxrb", h), G[h].at[1, 4:8])
+        recv(("gxlb", h), G[h].at[2, 0:4])
         recv(("gxr2", h), G[h].at[3, 0:4])
         recv(("gxl2", h), G[h].at[3, 4:8])
 
@@ -235,24 +246,28 @@
     def whole(h, k):
         return jnp.concatenate([HH[h][k, j * NT[h] : (j + 1) * NT[h], :] for j in range(3)], axis=1)
 
-    def input_grad(h):
-        ggp, gup = whole(h, 0), whole(h, 1)
+    def input_grad(h, half):
+        r, start = slice(half * NT[h] // 2, (half + 1) * NT[h] // 2), half * NT[h] * 4
+        ggp, gup = whole(h, 0)[r], whole(h, 1)[r]
         for n in range(4):
-            r = slice(n * 256, (n + 1) * 256)
-            part = nt(ggp, wg[r, :]) + nt(gup, wu[r, :])
+            w = slice(n * 256, (n + 1) * 256)
+            part = nt(ggp, wg[w, :]) + nt(gup, wu[w, :])
             for q in range(2):
-                T[h][pl.ds(n * 2 + q, NT[h], stride=8), :] = part[:, q * 128 : (q + 1) * 128]
+                T[h][pl.ds(start + n * 2 + q, NT[h] // 2, stride=8), :] = part[:, q * 128 : (q + 1) * 128]
 
     def slab(h, p, lo, hi):
         n = 24 * NB[h]
         return T[h][(p * 8 + lo) * n : (p * 8 + hi) * n, :].reshape(hi - lo, n, 128)
 
     def sum_x(h):
+        input_grad(h, 1)
         TB[h][3] = slab(h, 3, 0, 8).astype(BF)
         send(("x2r", h), TB[h].at[3, 0:4], RXa[h], right)
         send(("x2l", h), TB[h].at[3, 4:8], RXb[h], left)
+        input_grad(h, 0)
         TB[h][2, 4:8] = slab(h, 2, 4, 8).astype(BF)
         TB[h][1, 0:4] = slab(h, 1, 0, 4).astype(BF)
+        gone(2)
         send(("x1r", h), TB[h].at[2, 4:8], RX1[h].at[4:8], right)
         send(("x1l", h), TB[h].at[1, 0:4], RX2[h].at[0:4], left)
 
@@ -305,10 +320,12 @@
         recv(("gz", d), G[1].at[0, 0, d - 1])
     spread_y(1)
     spread_x(0)
+    spread_x2(0)
     forward(0)
+    spread_x(1)
     gathered(0)
     hand(0)
-    spread_x(1)
+    spread_x2(1)
     chip_sum(0)
     forward(1)
     middle(0)
@@ -318,7 +335,6 @@
     spread(0)
     chip_sum(1)
     collect(0)
-    input_grad(0)
     sum_x(0)
     sum_x2(0)
     middle(1)
@@ -327,7 +343,6 @@
     spread(1)
     give(2)
     collect(1)
-    input_grad(1)
     sum_x(1)
     own_sum = summed_y(0)
     fin[0:24, 0:128] = own_sum

time: 80.4 us -> 77.3 us (0.961)
  Pallas kernels: 79.5 us -> 76.4 us
    pallas_call x1, Pallas kernels: 77 us -> 73.9 us  [local(): pl.pallas_call(kernel, out_shape=shapes, in_specs=[far] * 8, out_specs=(v...]
where the time goes in v3:
time: 77.3 us; the launch traced here: 77.1 us
  Pallas kernels  76.4 us (99%)
    pallas_call x1, Pallas kernels, local(): pl.pallas_call(kernel, out_shape=shapes, in_specs=[far] * 8, out_specs=(v...  73.9 us
    pallas_call x1, Pallas kernels, local(): pl.pallas_call(copies, out_shape=shapes, in_specs=[hbm] * 4, out_specs=(f...  2.53 us

profile of v3, /device:TPU:2, one launch (start us, length us, event | category | flops | bytes accessed | tf_op | source)
XLA Modules:
  0.0 77.1 jit_solution(15282400335938172616)
XLA Ops:
  0.6 73.9 %shard_map.111 = (bf16[3,1024]{1,0:T(4,128)(2,1)}, bf16[1024,384]{1,0:T(8,128)(2,1)}, bf16[1024,384]{1,0:T(8,128)(2,1)}, bf16[384,1024]{1,0:T(8,128)(2,1)}) custom-call(bf16[3,1024]{1,0:T(4,128)(2,1)} %tok_in.1, bf16[3,1024]{1,0:T(4,128)(2,1)} %gout_in.1, bf16[1024,384]{1,0:T(8,128)(2,1)} %gc.1, f32[3,8]{1,0:T(4,128)} %bitcast.2, bf16[1024,384]{1,0:T(8,128)(2,1)} %uc.1, ...), custom_call_target="tpu_custom_call" | custom-call | tf_op jit(solution)/shard_map/pallas_call | solution.py:443
  74.5 2.5 %shard_map.112 = (bf16[3,1024]{1,0:T(4,128)(2,1)}, bf16[1024,384]{1,0:T(8,128)(2,1)}, bf16[1024,384]{1,0:T(8,128)(2,1)}, bf16[384,1024]{1,0:T(8,128)(2,1)}) custom-call(bf16[3,1024]{1,0:T(4,128)(2,1)} %get-tuple-element.8.refs_0_, bf16[1024,384]{1,0:T(8,128)(2,1)} %get-tuple-element.9.refs_1_, bf16[1024,384]{1,0:T(8,128)(2,1)} %get-tuple-element.10.refs_2_, ...), custom_call_target="tpu_custom_call" | custom-call | tf_op jit(solution)/shard_map/pallas_call | solution.py:465

commit v4 on v3

--- a/solution.py
+++ b/solution.py
@@ -33,10 +33,12 @@
     for _d in range(1, NY):
         _id("gy", _h, _d)
         _id("sy", _h, _d)
-    for _k in ("gxr", "gxl", "gxr2", "gxl2", "gxrb", "gxlb", "core", "x2r", "x2l", "x1r", "x1l", "xcr", "xcl"):
+    for _k in ("gxr", "gxl", "gxr2", "gxl2", "gxrb", "gxlb", "x2r", "x2l", "x1r", "x1l", "xcr", "xcl"):
         _id(_k, _h)
-    for _d in range(1, NZ):
-        _id("z", _h, _d)
+    for _k in range(3):
+        _id("core", _h, _k)
+        for _d in range(1, NZ):
+            _id("z", _h, _k, _d)
 for _k in range(3):
     for _d in range(NZ):
         _id("back", _k, _d)
@@ -96,8 +98,8 @@
 
     barrier = pltpu.get_barrier_semaphore()
     partners = (
-        [dev(y=up(y, d, NY)) for d in range(1, NY)]
-        + [dev(zh=up(zh, d, 3)) for d in (1, 2)]
+        [dev(zh=up(zh, d, 3)) for d in (1, 2)]
+        + [dev(y=up(y, d, NY)) for d in (4, 3, 5, 2, 6, 1, 7)]
         + [dev(x=up(x, d, NX)) for d in (1, 3)]
         + [dev(z=up(z, d, NZ)) for d in range(1, NZ)]
         + [dev(core=1 - core)]
@@ -183,33 +185,33 @@
         return pl.ds(pl.multiple_of(start, 16), n)
 
     def hand(h):
+        def cross(k, part):
+            put(h, k, part)
+            UB[h][k] = U[h][k, rows((1 - core) * HALF[h], HALF[h]), :].astype(BF)
+            send(("core", h, k), UB[h].at[k], RA[h].at[k], other)
+
         unpack(h, 0)
-        put(h, 0, jnp.dot(X[0, tokens_of(h), :], wg[...], preferred_element_type=F32))
-        put(h, 1, jnp.dot(X[0, tokens_of(h), :], wu[...], preferred_element_type=F32))
+        cross(0, jnp.dot(X[0, tokens_of(h), :], wg[...], preferred_element_type=F32))
+        cross(1, jnp.dot(X[0, tokens_of(h), :], wu[...], preferred_element_type=F32))
         unpack(h, 1)
-        put(h, 2, nt(X[1, tokens_of(h), :], wd[...]))
+        cross(2, nt(X[1, tokens_of(h), :], wd[...]))
+
+    def chip_sum(h):
         for k in range(3):
-            UB[h][k] = U[h][k, rows((1 - core) * HALF[h], HALF[h]), :].astype(BF)
-        send(("core", h), UB[h], RA[h], other)
-
-    def chip_sum(h):
-        recv(("core", h), RA[h])
-        for k in range(3):
+            recv(("core", h, k), RA[h].at[k])
             S[h][k] = (U[h][k, rows(core * HALF[h], HALF[h]), :] + RA[h][k].astype(F32)).astype(BF)
-        for d in (2, 1, 3):
-            zz = up(z, d, NZ)
-            send(("z", h, d), S[h].at[:, rows(zz * SEG[h], SEG[h])], RB[h].at[d - 1], dev(z=zz))
+            for d in (2, 1, 3):
+                zz = up(z, d, NZ)
+                send(("z", h, k, d), S[h].at[k, rows(zz * SEG[h], SEG[h])], RB[h].at[d - 1, k], dev(z=zz))
 
     def share(h, zz, cc):
         return rows(cc * HALF[h] + zz * SEG[h], SEG[h])
 
     def middle(h):
-        for d in range(1, NZ):
-            recv(("z", h, d), RB[h].at[d - 1])
-
         def total(k):
             t = U[h][k, share(h, z, core), :] + RA[h][k, rows(z * SEG[h], SEG[h]), :].astype(F32)
             for d in range(1, NZ):
+                recv(("z", h, k, d), RB[h].at[d - 1, k])
                 t = t + RB[h][d - 1, k].astype(F32)
             return t
 
@@ -375,13 +377,13 @@
 
     v = summed_y(1)
     for i in range(2):
-        ZB[i] = v[i * 24 : (i + 1) * 24, :]
+        ZB[i] = v[i * 24 : (i + 1) * 24, :].astype(BF)
     for d in (1, 2):
         send(("sz", d), ZB.at[d - 1], RZ.at[d - 1], dev(zh=up(zh, -d, 3)))
     v = fin[0:24, 0:128]
     for d in (1, 2):
         recv(("sz", d), RZ.at[d - 1])
-        v = v + RZ[d - 1]
+        v = v + RZ[d - 1].astype(F32)
     for r in range(3):
         for c in range(8):
             fin[r : r + 1, c * 128 : (c + 1) * 128] = v[r * 8 + c : r * 8 + c + 1, :]
@@ -452,7 +454,7 @@
             V((2, TOK, FEAT), BF),
             V((FEAT, HID), BF), V((FEAT, HID), BF), V((HID, FEAT), BF),
             V((24, FEAT), F32),
-            V((2, 24, 128), F32), V((2, 24, 128), F32),
+            V((2, 24, 128), BF), V((2, 24, 128), BF),
             *chunk_scratch(0), *chunk_scratch(1),
             pltpu.SemaphoreType.DMA((11,)),
             pltpu.SemaphoreType.DMA((N_IDS,)),

time: 77.3 us -> 77.2 us (level)
  no operation moved by 1% of the time
where the time goes in v4:
time: 77.2 us; the launch traced here: 76.9 us
  Pallas kernels  76.3 us (99%)
    pallas_call x1, Pallas kernels, local(): pl.pallas_call(kernel, out_shape=shapes, in_specs=[far] * 8, out_specs=(v...  73.7 us
    pallas_call x1, Pallas kernels, local(): pl.pallas_call(copies, out_shape=shapes, in_specs=[hbm] * 4, out_specs=(f...  2.53 us

profile of v4, /device:TPU:2, one launch (start us, length us, event | category | flops | bytes accessed | tf_op | source)
XLA Modules:
  0.0 76.9 jit_solution(12028068563176553029)
XLA Ops:
  0.6 73.7 %shard_map.111 = (bf16[3,1024]{1,0:T(4,128)(2,1)}, bf16[1024,384]{1,0:T(8,128)(2,1)}, bf16[1024,384]{1,0:T(8,128)(2,1)}, bf16[384,1024]{1,0:T(8,128)(2,1)}) custom-call(bf16[3,1024]{1,0:T(4,128)(2,1)} %tok_in.1, bf16[3,1024]{1,0:T(4,128)(2,1)} %gout_in.1, bf16[1024,384]{1,0:T(8,128)(2,1)} %gc.1, f32[3,8]{1,0:T(4,128)} %bitcast.2, bf16[1024,384]{1,0:T(8,128)(2,1)} %uc.1, ...), custom_call_target="tpu_custom_call" | custom-call | tf_op jit(solution)/shard_map/pallas_call | solution.py:445
  74.4 2.5 %shard_map.112 = (bf16[3,1024]{1,0:T(4,128)(2,1)}, bf16[1024,384]{1,0:T(8,128)(2,1)}, bf16[1024,384]{1,0:T(8,128)(2,1)}, bf16[384,1024]{1,0:T(8,128)(2,1)}) custom-call(bf16[3,1024]{1,0:T(4,128)(2,1)} %get-tuple-element.8.refs_0_, bf16[1024,384]{1,0:T(8,128)(2,1)} %get-tuple-element.9.refs_1_, bf16[1024,384]{1,0:T(8,128)(2,1)} %get-tuple-element.10.refs_2_, ...), custom_call_target="tpu_custom_call" | custom-call | tf_op jit(solution)/shard_map/pallas_call | solution.py:467

commit v5 on v4

--- a/solution.py
+++ b/solution.py
@@ -39,7 +39,7 @@
         _id("core", _h, _k)
         for _d in range(1, NZ):
             _id("z", _h, _k, _d)
-for _k in range(3):
+for _k in range(4):
     for _d in range(NZ):
         _id("back", _k, _d)
         _id("backcore", _k, _d)
@@ -223,7 +223,7 @@
         HH[h][1, at, :] = (grad_hidden * act).astype(BF)
         HH[h][2, at, :] = (act * up_value).astype(BF)
 
-    groups = ((0, 0, 3), (1, 0, 2), (1, 2, 1))
+    groups = ((0, 0, 3), (1, 0, 1), (1, 1, 1), (1, 2, 1))
 
     def piece(g, zz, cc):
         h, lo, n = groups[g]
@@ -341,15 +341,18 @@
     sum_x2(0)
     middle(1)
     give(1)
+    give(2)
     sum_y(0)
     spread(1)
-    give(2)
+    spread(2)
+    give(3)
     collect(1)
+    collect(2)
     sum_x(1)
     own_sum = summed_y(0)
     fin[0:24, 0:128] = own_sum
     sum_x2(1)
-    spread(2)
+    spread(3)
 
     both = jnp.concatenate(
         [jnp.concatenate([whole(h, 0), whole(h, 1)], axis=1) for h in range(2)], axis=0
@@ -368,7 +371,7 @@
     weight_grads(3)
     store(og, gg)
     store(ou, gu)
-    collect(2)
+    collect(3)
     hid = jnp.concatenate([whole(0, 2), whole(1, 2)], axis=0)
     for n in range(3):
         r = slice(n * 128, (n + 1) * 128)

time: 77.2 us -> 77.4 us (level)
  no operation moved by 1% of the time
where the time goes in v5:
time: 77.4 us; the launch traced here: 77.1 us
  Pallas kernels  76.5 us (99%)
    pallas_call x1, Pallas kernels, local(): pl.pallas_call(kernel, out_shape=shapes, in_specs=[far] * 8, out_specs=(v...  74 us
    pallas_call x1, Pallas kernels, local(): pl.pallas_call(copies, out_shape=shapes, in_specs=[hbm] * 4, out_specs=(f...  2.53 us

profile of v5, /device:TPU:2, one launch (start us, length us, event | category | flops | bytes accessed | tf_op | source)
XLA Modules:
  0.0 77.1 jit_solution(8501864921285806394)
XLA Ops:
  0.6 74.0 %shard_map.111 = (bf16[3,1024]{1,0:T(4,128)(2,1)}, bf16[1024,384]{1,0:T(8,128)(2,1)}, bf16[1024,384]{1,0:T(8,128)(2,1)}, bf16[384,1024]{1,0:T(8,128)(2,1)}) custom-call(bf16[3,1024]{1,0:T(4,128)(2,1)} %tok_in.1, bf16[3,1024]{1,0:T(4,128)(2,1)} %gout_in.1, bf16[1024,384]{1,0:T(8,128)(2,1)} %gc.1, f32[3,8]{1,0:T(4,128)} %bitcast.2, bf16[1024,384]{1,0:T(8,128)(2,1)} %uc.1, ...), custom_call_target="tpu_custom_call" | custom-call | tf_op jit(solution)/shard_map/pallas_call | solution.py:448
  74.6 2.5 %shard_map.112 = (bf16[3,1024]{1,0:T(4,128)(2,1)}, bf16[1024,384]{1,0:T(8,128)(2,1)}, bf16[1024,384]{1,0:T(8,128)(2,1)}, bf16[384,1024]{1,0:T(8,128)(2,1)}) custom-call(bf16[3,1024]{1,0:T(4,128)(2,1)} %get-tuple-element.8.refs_0_, bf16[1024,384]{1,0:T(8,128)(2,1)} %get-tuple-element.9.refs_1_, bf16[1024,384]{1,0:T(8,128)(2,1)} %get-tuple-element.10.refs_2_, ...), custom_call_target="tpu_custom_call" | custom-call | tf_op jit(solution)/shard_map/pallas_call | solution.py:470
